TPU v7x, 32 devices: a whole 2x2x4 slice. The times are simulated.
32 devices in a mesh: dp: 32 (over z, y, x, core).
Axes of the slice: x: 2, y: 2, z: 4, core: 2. Of those that a mesh axis runs over, the one named last changes fastest.
Arguments:
- inputs: bfloat16 [64, 1024, 576], P('dp'), may hold values from -6 to 6
- cotangent: bfloat16 [64, 1024, 576], P('dp'), may hold values from -6 to 6
- segments: int32 [64, 1024], P('dp'), may hold values from 0 to 2, as said below
- norm_gains: float32 [2, 576], replicated, may hold values from 0.5 to 1.5
- query_weight: float32 [331776], P('dp'), may hold values from -0.25 to 0.25
- key_weight: float32 [110592], P('dp'), may hold values from -0.25 to 0.25
- value_weight: float32 [110592], P('dp'), may hold values from -0.25 to 0.25
- out_weight: float32 [331776], P('dp'), may hold values from -0.75 to 0.75
- gate_weight: float32 [884736], P('dp'), may hold values from -0.25 to 0.25
- up_weight: float32 [884736], P('dp'), may hold values from -0.25 to 0.25
- down_weight: float32 [884736], P('dp'), may hold values from -0.15625 to 0.15625
- query_first: float32 [331776], P('dp'), may hold values from -256 to 256
- key_first: float32 [110592], P('dp'), may hold values from -256 to 256
- value_first: float32 [110592], P('dp'), may hold values from -256 to 256
- out_first: float32 [331776], P('dp'), may hold values from -64 to 64
- gate_first: float32 [884736], P('dp'), may hold values from -64 to 64
- up_first: float32 [884736], P('dp'), may hold values from -64 to 64
- down_first: float32 [884736], P('dp'), may hold values from -96 to 96
- query_second: float32 [331776], P('dp'), may hold values from 7864.32 to 31457.28
- key_second: float32 [110592], P('dp'), may hold values from 7864.32 to 31457.28
- value_second: float32 [110592], P('dp'), may hold values from 7864.32 to 31457.28
- out_second: float32 [331776], P('dp'), may hold values from 458.752 to 1835.008
- gate_second: float32 [884736], P('dp'), may hold values from 458.752 to 1835.008
- up_second: float32 [884736], P('dp'), may hold values from 458.752 to 1835.008
- down_second: float32 [884736], P('dp'), may hold values from 1245.184 to 4980.736
- gain_first: float32 [2, 576], replicated, may hold values from -224 to 224
- gain_second: float32 [2, 576], replicated, may hold values from 2621.44 to 13107.2
Outputs:
- outputs: bfloat16 [64, 1024, 576], P('dp')
- input_grad: float32 [64, 1024, 576], P('dp')
- query_grad: float32 [331776], P('dp')
- query_moment: float32 [331776], P('dp')
- query_new: float32 [331776], P('dp')
- key_grad: float32 [110592], P('dp')
- key_moment: float32 [110592], P('dp')
- key_new: float32 [110592], P('dp')
- value_grad: float32 [110592], P('dp')
- value_moment: float32 [110592], P('dp')
- value_new: float32 [110592], P('dp')
- out_grad: float32 [331776], P('dp')
- out_moment: float32 [331776], P('dp')
- out_new: float32 [331776], P('dp')
- gate_grad: float32 [884736], P('dp')
- gate_moment: float32 [884736], P('dp')
- gate_new: float32 [884736], P('dp')
- up_grad: float32 [884736], P('dp')
- up_moment: float32 [884736], P('dp')
- up_new: float32 [884736], P('dp')
- down_grad: float32 [884736], P('dp')
- down_moment: float32 [884736], P('dp')
- down_new: float32 [884736], P('dp')
- gain_grad: float32 [2, 576], replicated
- gain_moment: float32 [2, 576], replicated
- gains_new: float32 [2, 576], replicated
Inputs may be any that keep to these rules, and one draw needn't show every extreme that they name: `segments`: in each sequence the segment numbers start at 0, never fall, and rise by one at each of two places: the first segment holds 64 to 511 tokens, the second 1024 // 5 to 511.
All inputs are finite; a program needn't handle non-finite values.
Results may differ from a plain program's by a relative error of at most 0.013.
Values may be sent and summed in bfloat16 or wider, within the bound.
A program may use at most 320 MiB of HBM per device.

v0:
```python
import jax
import jax.numpy as jnp
from jax import lax
from jax.sharding import PartitionSpec as P

D = 576
HEADS = 9
KV_HEADS = 3
HEAD = 64
FF = 1536
MICRO = 2
STEP = 10


norm_eps = 1e-05
rope_base = 100000.0
learn_rate = 0.06
gain_rate = 0.4
beta_first = 0.9
beta_second = 0.95
adam_eps = 1e-08
decay_rate = 0.1


def rms_scale(values, gain):
    return values * lax.rsqrt(jnp.mean(values * values, axis=-1, keepdims=True) + norm_eps) * gain


def doc_positions(segments):
    places = jnp.arange(segments.shape[-1], dtype=jnp.int32)
    first_col = jnp.ones(segments.shape[:-1] + (1,), dtype=jnp.bool_)
    change = jnp.concatenate([first_col, segments[..., 1:] != segments[..., :-1]], axis=-1)
    starts = lax.cummax(jnp.where(change, places, jnp.zeros_like(places)), axis=segments.ndim - 1)
    return places - starts


def rope_tables(positions):
    half_size = HEAD // 2
    frequency = rope_base ** (-(jnp.arange(half_size, dtype=jnp.float32) * 2.0 / HEAD))
    angles = positions.astype(jnp.float32)[..., None] * frequency
    return (jnp.cos(angles), jnp.sin(angles))


def rotate(values, cosine_part, sine_part):
    half_size = values.shape[-1] // 2
    first_half = values[..., :half_size]
    second_half = values[..., half_size:]
    cos_rows = cosine_part[..., None, :]
    sin_rows = sine_part[..., None, :]
    return jnp.concatenate(
        [
            first_half * cos_rows - second_half * sin_rows,
            second_half * cos_rows + first_half * sin_rows,
        ],
        axis=-1,
    )


def matmul(left, right):
    return jnp.dot(left, right, preferred_element_type=jnp.float32)


def left_dot(left, right):
    return lax.dot_general(
        left, right, (((0,), (0,)), ((), ())), preferred_element_type=jnp.float32
    )


def right_dot(left, right):
    return lax.dot_general(
        left, right, (((1,), (1,)), ((), ())), preferred_element_type=jnp.float32
    )


def norm_back(values, gain, upstream):
    normed_out, pull_back = jax.vjp(rms_scale, values, gain)
    return pull_back(upstream)


def block_allowed(seg_rows, offset, block_rows):
    places = jnp.arange(seg_rows.shape[1], dtype=jnp.int32)
    same_doc = seg_rows[:, offset : offset + block_rows, None] == seg_rows[:, None, :]
    causal = places[offset : offset + block_rows, None] >= places[None, :]
    return jnp.logical_and(same_doc, causal)[:, None, None, :, :]


def attention_forward(query_rows, key_rows, value_rows, seg_rows):
    seq_len = query_rows.shape[1]
    block_rows = min(512, seq_len)
    score_scale = query_rows.shape[-1] ** (-0.5)
    outputs_list = []
    log_list = []
    for offset in range(0, seq_len, block_rows):
        query_block = query_rows[:, offset : offset + block_rows]
        allowed = block_allowed(seg_rows, offset, block_rows)
        raw_scores = jnp.einsum(
            "nqkgd,nskd->nkgqs", query_block, key_rows, preferred_element_type=jnp.float32
        )
        scaled = jnp.where(allowed, raw_scores * score_scale, -1e30)
        top_score = jnp.max(scaled, axis=-1, keepdims=True)
        exp_terms = jnp.where(allowed, jnp.exp(scaled - top_score), 0.0)
        row_total = jnp.sum(exp_terms, axis=-1, keepdims=True)
        attn_probs = (exp_terms / row_total).astype(jnp.bfloat16)
        outputs_list.append(
            jnp.einsum(
                "nkgqs,nskd->nqkgd", attn_probs, value_rows, preferred_element_type=jnp.float32
            )
        )
        log_list.append(top_score + jnp.log(row_total))
    return (jnp.concatenate(outputs_list, axis=1), log_list)


def attention_backward(query_rows, key_rows, value_rows, seg_rows, log_list, out_back):
    seq_len = query_rows.shape[1]
    block_rows = min(512, seq_len)
    score_scale = query_rows.shape[-1] ** (-0.5)
    key_back = jnp.zeros(key_rows.shape, jnp.float32)
    value_back = jnp.zeros(value_rows.shape, jnp.float32)
    query_list = []
    for block_index, offset in enumerate(range(0, seq_len, block_rows)):
        query_block = query_rows[:, offset : offset + block_rows]
        back_block = out_back[:, offset : offset + block_rows]
        allowed = block_allowed(seg_rows, offset, block_rows)
        raw_scores = jnp.einsum(
            "nqkgd,nskd->nkgqs", query_block, key_rows, preferred_element_type=jnp.float32
        )
        scaled = jnp.where(allowed, raw_scores * score_scale, -1e30)
        probs_full = jnp.where(allowed, jnp.exp(scaled - log_list[block_index]), 0.0)
        attn_probs = probs_full.astype(jnp.bfloat16)
        value_back = value_back + jnp.einsum(
            "nkgqs,nqkgd->nskd", attn_probs, back_block, preferred_element_type=jnp.float32
        )
        prob_back = jnp.einsum(
            "nqkgd,nskd->nkgqs", back_block, value_rows, preferred_element_type=jnp.float32
        )
        delta_rows = jnp.sum(probs_full * prob_back, axis=-1, keepdims=True)
        score_back = (probs_full * (prob_back - delta_rows) * score_scale).astype(jnp.bfloat16)
        query_list.append(
            jnp.einsum(
                "nkgqs,nskd->nqkgd", score_back, key_rows, preferred_element_type=jnp.float32
            )
        )
        key_back = key_back + jnp.einsum(
            "nkgqs,nqkgd->nskd", score_back, query_block, preferred_element_type=jnp.float32
        )
    return (jnp.concatenate(query_list, axis=1), key_back, value_back)


def forward_pass(x_micro, seg_micro, matrices, gain_pair):
    query_mat, key_mat, value_mat, out_mat, gate_mat, up_mat, down_mat = matrices
    seq_count, seq_len = (x_micro.shape[0], x_micro.shape[1])
    tokens_flat = x_micro.reshape(seq_count * seq_len, D).astype(jnp.float32)
    cosine_part, sine_part = rope_tables(doc_positions(seg_micro))
    normed = rms_scale(tokens_flat, gain_pair[0]).astype(jnp.bfloat16)
    query_lin = matmul(normed, query_mat).reshape(seq_count, seq_len, HEADS, HEAD)
    query_rows = (
        rotate(query_lin, cosine_part, sine_part)
        .astype(jnp.bfloat16)
        .reshape(seq_count, seq_len, KV_HEADS, HEADS // KV_HEADS, HEAD)
    )
    key_lin = matmul(normed, key_mat).reshape(seq_count, seq_len, KV_HEADS, HEAD)
    key_rows = rotate(key_lin, cosine_part, sine_part).astype(jnp.bfloat16)
    value_rows = (
        matmul(normed, value_mat).astype(jnp.bfloat16).reshape(seq_count, seq_len, KV_HEADS, HEAD)
    )
    attended, log_list = attention_forward(query_rows, key_rows, value_rows, seg_micro)
    attn_rows = attended.reshape(seq_count * seq_len, HEADS * HEAD).astype(jnp.bfloat16)
    middle = tokens_flat + matmul(attn_rows, out_mat)
    normed2 = rms_scale(middle, gain_pair[1]).astype(jnp.bfloat16)
    gate_lin = matmul(normed2, gate_mat)
    up_lin = matmul(normed2, up_mat)
    hidden = (jax.nn.silu(gate_lin) * up_lin).astype(jnp.bfloat16)
    result = (middle + matmul(hidden, down_mat)).astype(jnp.bfloat16).reshape(x_micro.shape)
    saved_parts = (
        tokens_flat,
        normed,
        query_rows,
        key_rows,
        value_rows,
        seg_micro,
        log_list,
        attn_rows,
        middle,
        normed2,
        gate_lin,
        up_lin,
        hidden,
        cosine_part,
        sine_part,
    )
    return (saved_parts, result)


def backward_pass(saved_parts, back_micro, matrices, gain_pair):
    (
        tokens_flat,
        normed,
        query_rows,
        key_rows,
        value_rows,
        seg_micro,
        log_list,
        attn_rows,
        middle,
        normed2,
        gate_lin,
        up_lin,
        hidden,
        cosine_part,
        sine_part,
    ) = saved_parts
    query_mat, key_mat, value_mat, out_mat, gate_mat, up_mat, down_mat = matrices
    seq_count, seq_len = (query_rows.shape[0], query_rows.shape[1])
    back_rows = back_micro.reshape(seq_count * seq_len, D)
    down_grad = left_dot(hidden, back_rows)
    hidden_back = right_dot(back_rows, down_mat)
    gate_sig = jax.nn.sigmoid(gate_lin)
    gate_back = (hidden_back * up_lin * gate_sig * (1.0 + gate_lin * (1.0 - gate_sig))).astype(
        jnp.bfloat16
    )
    up_back = (hidden_back * gate_lin * gate_sig).astype(jnp.bfloat16)
    gate_grad = left_dot(normed2, gate_back)
    up_grad = left_dot(normed2, up_back)
    normed2_back = right_dot(gate_back, gate_mat) + right_dot(up_back, up_mat)
    middle_part, gain_two = norm_back(middle, gain_pair[1], normed2_back)
    middle_back = back_rows.astype(jnp.float32) + middle_part
    branch_back = middle_back.astype(jnp.bfloat16)
    out_grad = left_dot(attn_rows, branch_back)
    attn_back = right_dot(branch_back, out_mat).astype(jnp.bfloat16).reshape(query_rows.shape)
    query_back, key_back, value_back = attention_backward(
        query_rows, key_rows, value_rows, seg_micro, log_list, attn_back
    )
    query_back = (
        rotate(query_back.reshape(seq_count, seq_len, HEADS, HEAD), cosine_part, -sine_part)
        .astype(jnp.bfloat16)
        .reshape(seq_count * seq_len, HEADS * HEAD)
    )
    key_back = (
        rotate(key_back, cosine_part, -sine_part)
        .astype(jnp.bfloat16)
        .reshape(seq_count * seq_len, KV_HEADS * HEAD)
    )
    value_back = value_back.astype(jnp.bfloat16).reshape(seq_count * seq_len, KV_HEADS * HEAD)
    query_grad = left_dot(normed, query_back)
    key_grad = left_dot(normed, key_back)
    value_grad = left_dot(normed, value_back)
    normed_back = (
        right_dot(query_back, query_mat)
        + right_dot(key_back, key_mat)
        + right_dot(value_back, value_mat)
    )
    input_part, gain_one = norm_back(tokens_flat, gain_pair[0], normed_back)
    input_back = middle_back + input_part
    weight_back = (query_grad, key_grad, value_grad, out_grad, gate_grad, up_grad, down_grad)
    return (input_back, weight_back, jnp.stack([gain_one, gain_two]))


def adam_step(weight_now, gradient, moment_one, moment_two, step_rate, decay_value):
    one_new = beta_first * moment_one + (1.0 - beta_first) * gradient
    two_new = beta_second * moment_two + (1.0 - beta_second) * gradient * gradient
    fix_first = 1.0 - beta_first**STEP
    fix_second = 1.0 - beta_second**STEP
    weight_new = weight_now - step_rate * (
        one_new / fix_first / (jnp.sqrt(two_new / fix_second) + adam_eps) + decay_value * weight_now
    )
    return (two_new, weight_new)


def body(
    inputs,
    cotangent,
    segments,
    norm_gains,
    query_weight,
    key_weight,
    value_weight,
    out_weight,
    gate_weight,
    up_weight,
    down_weight,
    query_first,
    key_first,
    value_first,
    out_first,
    gate_first,
    up_first,
    down_first,
    query_second,
    key_second,
    value_second,
    out_second,
    gate_second,
    up_second,
    down_second,
    gain_first,
    gain_second,
):
    query_cols = HEADS * HEAD
    pair_cols = KV_HEADS * HEAD
    shapes = (
        (D, query_cols),
        (D, pair_cols),
        (D, pair_cols),
        (query_cols, D),
        (D, FF),
        (D, FF),
        (FF, D),
    )
    masters = (
        query_weight,
        key_weight,
        value_weight,
        out_weight,
        gate_weight,
        up_weight,
        down_weight,
    )
    firsts = (query_first, key_first, value_first, out_first, gate_first, up_first, down_first)
    seconds = (
        query_second,
        key_second,
        value_second,
        out_second,
        gate_second,
        up_second,
        down_second,
    )
    low_shards = tuple((master.astype(jnp.bfloat16) for master in masters))

    def unflatten(flat_list):
        return tuple(
            (flat_part.reshape(shape_pair) for flat_part, shape_pair in zip(flat_list, shapes))
        )

    per_micro = inputs.shape[0] // MICRO
    weight_totals = tuple((jnp.zeros(shape_pair, jnp.float32) for shape_pair in shapes))
    shard_sums = tuple((jnp.zeros(master.shape, jnp.float32) for master in masters))
    gain_totals = jnp.zeros((2, D), jnp.float32)
    result_list = []
    input_list = []
    for micro_index in range(MICRO):
        row_start = micro_index * per_micro
        row_stop = row_start + per_micro
        forward_mats = unflatten(
            (
                lax.all_gather(low_shards[0], "dp", axis=0, tiled=True),
                lax.all_gather(low_shards[1], "dp", axis=0, tiled=True),
                lax.all_gather(low_shards[2], "dp", axis=0, tiled=True),
                lax.all_gather(low_shards[3], "dp", axis=0, tiled=True),
                lax.all_gather(low_shards[4], "dp", axis=0, tiled=True),
                lax.all_gather(low_shards[5], "dp", axis=0, tiled=True),
                lax.all_gather(low_shards[6], "dp", axis=0, tiled=True),
            )
        )
        saved_parts, result = forward_pass(
            inputs[row_start:row_stop], segments[row_start:row_stop], forward_mats, norm_gains
        )
        backward_mats = unflatten(
            (
                lax.all_gather(low_shards[0], "dp", axis=0, tiled=True),
                lax.all_gather(low_shards[1], "dp", axis=0, tiled=True),
                lax.all_gather(low_shards[2], "dp", axis=0, tiled=True),
                lax.all_gather(low_shards[3], "dp", axis=0, tiled=True),
                lax.all_gather(low_shards[4], "dp", axis=0, tiled=True),
                lax.all_gather(low_shards[5], "dp", axis=0, tiled=True),
                lax.all_gather(low_shards[6], "dp", axis=0, tiled=True),
            )
        )
        input_back, weight_back, gain_back = backward_pass(
            saved_parts, cotangent[row_start:row_stop], backward_mats, norm_gains
        )
        result_list.append(result)
        input_list.append(input_back.reshape(result.shape))
        gain_totals = gain_totals + gain_back
        weight_totals = tuple(
            (total_part + new_part for total_part, new_part in zip(weight_totals, weight_back))
        )
    shard_sums = (
        lax.psum_scatter(weight_totals[0].reshape(-1), "dp", scatter_dimension=0, tiled=True),
        lax.psum_scatter(weight_totals[1].reshape(-1), "dp", scatter_dimension=0, tiled=True),
        lax.psum_scatter(weight_totals[2].reshape(-1), "dp", scatter_dimension=0, tiled=True),
        lax.psum_scatter(weight_totals[3].reshape(-1), "dp", scatter_dimension=0, tiled=True),
        lax.psum_scatter(weight_totals[4].reshape(-1), "dp", scatter_dimension=0, tiled=True),
        lax.psum_scatter(weight_totals[5].reshape(-1), "dp", scatter_dimension=0, tiled=True),
        lax.psum_scatter(weight_totals[6].reshape(-1), "dp", scatter_dimension=0, tiled=True),
    )
    gain_sum = lax.psum(gain_totals, "dp")
    results = [jnp.concatenate(result_list, axis=0), jnp.concatenate(input_list, axis=0)]
    for slot_index in range(7):
        gradient = shard_sums[slot_index]
        moment_new, weight_new = adam_step(
            masters[slot_index],
            gradient,
            firsts[slot_index],
            seconds[slot_index],
            learn_rate,
            decay_rate,
        )
        results.extend([gradient, moment_new, weight_new])
    gain_moment, gains_new = adam_step(
        norm_gains, gain_sum, gain_first, gain_second, gain_rate, 0.0
    )
    results.extend([gain_sum, gain_moment, gains_new])
    return tuple(results)


def solution(mesh):
    in_specs = (
        P("dp", None, None),
        P("dp", None, None),
        P("dp", None),
        P(),
        P("dp"),
        P("dp"),
        P("dp"),
        P("dp"),
        P("dp"),
        P("dp"),
        P("dp"),
        P("dp"),
        P("dp"),
        P("dp"),
        P("dp"),
        P("dp"),
        P("dp"),
        P("dp"),
        P("dp"),
        P("dp"),
        P("dp"),
        P("dp"),
        P("dp"),
        P("dp"),
        P("dp"),
        P(),
        P(),
    )
    out_specs = (
        P("dp", None, None),
        P("dp", None, None),
        P("dp"),
        P("dp"),
        P("dp"),
        P("dp"),
        P("dp"),
        P("dp"),
        P("dp"),
        P("dp"),
        P("dp"),
        P("dp"),
        P("dp"),
        P("dp"),
        P("dp"),
        P("dp"),
        P("dp"),
        P("dp"),
        P("dp"),
        P("dp"),
        P("dp"),
        P("dp"),
        P("dp"),
        P(),
        P(),
        P(),
    )
    return jax.shard_map(body, mesh=mesh, in_specs=in_specs, out_specs=out_specs, check_vma=False)
```

profile of v0, /device:TPU:0, one launch (start us, length us, event | category | flops | bytes accessed | tf_op | source)
XLA Modules:
  0.0 952.9 jit_solution(4052307222062944358)
XLA Ops:
  20.3 44.7 %all-gather = bf16[32,1,3456]{2,1,0:T(2,128)(2,1)S(1)} all-gather(bf16[1,1,3456]{2,1,0:T(2,128)(2,1)S(1)} %reshape.1678), channel_id=1, replica_groups=mesh['dp'=32] {'dp'}, dimensions={0}, use_global_device_ids=true | all-gather | bytes 228096 | tf_op jit(solution)/shard_map/all_gather | solution.py:348
  69.3 38.3 %all-gather.1 = bf16[32,1,3456]{2,1,0:T(2,128)(2,1)S(1)} all-gather(bf16[1,1,3456]{2,1,0:T(2,128)(2,1)S(1)} %reshape.1680), channel_id=1, replica_groups=mesh['dp'=32] {'dp'}, dimensions={0}, use_global_device_ids=true | all-gather | bytes 228096 | tf_op jit(solution)/shard_map/all_gather | solution.py:347
  112.3 44.7 %all-gather.2 = bf16[32,1,10368]{2,1,0:T(2,128)(2,1)} all-gather(bf16[1,1,10368]{2,1,0:T(2,128)(2,1)S(1)} %reshape.1682), channel_id=1, replica_groups=mesh['dp'=32] {'dp'}, dimensions={0}, use_global_device_ids=true | all-gather | bytes 684288 | tf_op jit(solution)/shard_map/all_gather | solution.py:346
  157.0 5.8 reduce.17
  174.1 42.9 %all-gather.3 = bf16[32,1,10368]{2,1,0:T(2,128)(2,1)S(1)} all-gather(bf16[1,1,10368]{2,1,0:T(2,128)(2,1)S(1)} %reshape.1684), channel_id=1, replica_groups=mesh['dp'=32] {'dp'}, dimensions={0}, use_global_device_ids=true | all-gather | bytes 684288 | tf_op jit(solution)/shard_map/all_gather | solution.py:349
  231.3 8.1 fusion.245
  239.4 8.1 fusion.246
  247.5 9.7 %fusion.17 = f32[3,3,512]{2,1,0:T(4,128)S(1)} fusion(f32[1,3,3,512,1024]{3,4,2,1,0:T(8,128)} %get-tuple-element.125, f32[3,3,512]{2,1,0:T(4,128)S(1)} %get-tuple-element.124, pred[512,1024]{0,1:T(8,128)(4,1)S(1)} %get-tuple-element.115), kind=kLoop, calls=%fused_computation.41 | loop fusion | flops 14151168 | bytes 19435520 | tf_op jit(solution)/shard_map/reduce_sum | solution.py:102
  257.2 10.0 %fusion.89 = bf16[3,64,3,512]{3,1,2,0:T(8,128)(2,1)} fusion(bf16[1024,3,64,1]{0,2,3,1:T(8,128)(2,1)S(1)} %bitcast.578, f32[3,3,512]{2,1,0:T(4,128)S(1)} %fusion.17, f32[1,3,3,512,1024]{3,4,2,1,0:T(8,128)} %get-tuple-element.125, f32[3,3,512]{2,1,0:T(4,128)S(1)} %get-tuple-element.124, pred[512,1024]{0,1:T(8,128)(4,1)S(1)} %get-tuple-element.115), kind=kOutput, calls=%fused_computation.156 | convolution fusion | flops 623149056 | bytes 20418560 | tf_op jit(solution)/shard_map/nkgqs,nskd->nqkgd/dot_general | solution.py:105
  267.3 9.7 %fusion.16 = f32[3,3,512]{2,1,0:T(4,128)S(1)} fusion(f32[1,3,3,512,1024]{3,4,2,1,0:T(8,128)} %get-tuple-element.127, f32[3,3,512]{2,1,0:T(4,128)S(1)} %get-tuple-element.126, pred[512,1024]{0,1:T(8,128)(4,1)S(1)} %get-tuple-element.116), kind=kLoop, calls=%fused_computation.40 | loop fusion | flops 14151168 | bytes 19435520 | tf_op jit(solution)/shard_map/reduce_sum | solution.py:102
  277.0 9.8 %fusion.86 = bf16[3,64,3,512]{3,1,2,0:T(8,128)(2,1)} fusion(bf16[1024,3,64,1]{0,2,3,1:T(8,128)(2,1)S(1)} %bitcast.579, f32[3,3,512]{2,1,0:T(4,128)S(1)} %fusion.16, f32[1,3,3,512,1024]{3,4,2,1,0:T(8,128)} %get-tuple-element.127, f32[3,3,512]{2,1,0:T(4,128)S(1)} %get-tuple-element.126, pred[512,1024]{0,1:T(8,128)(4,1)S(1)} %get-tuple-element.116), kind=kOutput, calls=%fused_computation.155 | convolution fusion | flops 623149056 | bytes 20418560 | tf_op jit(solution)/shard_map/nkgqs,nskd->nqkgd/dot_general | solution.py:105
  286.8 8.0 fusion.243
  294.9 8.4 fusion.244
  303.3 9.6 %fusion.19 = f32[3,3,512]{2,1,0:T(4,128)S(1)} fusion(f32[1,3,3,512,1024]{3,4,2,1,0:T(8,128)} %get-tuple-element.121, f32[3,3,512]{2,1,0:T(4,128)S(1)} %get-tuple-element.120, pred[512,1024]{0,1:T(8,128)(4,1)S(1)} %get-tuple-element.114), kind=kLoop, calls=%fused_computation.43 | loop fusion | flops 14151168 | bytes 19435520 | tf_op jit(solution)/shard_map/reduce_sum | solution.py:102
  312.9 8.9 fusion.95
  321.8 9.8 %fusion.18 = f32[3,3,512]{2,1,0:T(4,128)S(1)} fusion(f32[1,3,3,512,1024]{3,4,2,1,0:T(8,128)} %get-tuple-element.123, f32[3,3,512]{2,1,0:T(4,128)S(1)} %get-tuple-element.122, pred[512,1024]{0,1:T(8,128)(4,1)S(1)} %get-tuple-element.113), kind=kLoop, calls=%fused_computation.42 | loop fusion | flops 14151168 | bytes 19435520 | tf_op jit(solution)/shard_map/reduce_sum | solution.py:102
  331.7 9.1 fusion.92
  348.5 4.4 reshape.1625
  357.4 7.3 fusion.248
  364.7 4.6 fusion.247
  373.6 11.3 %multiply_convert_fusion.2 = (bf16[1024,1536]{1,0:T(8,128)(2,1)S(1)}, bf16[1024,1536]{1,0:T(8,128)(2,1)S(1)}, bf16[1024,1536]{1,0:T(8,128)(2,1)}) fusion(f32[1024,1536]{1,0:T(8,128)} %fusion.247, f32[1024,1536]{1,0:T(8,128)} %fusion.248, bf16[1536,576]{1,0:T(8,128)(2,1)} %reshape.1627, bf16[2,1024,576]{1,2,0:T(8,128)(2,1)} %param.28), kind=kOutput, calls=%fused_computation.74 | convolution fusion | flops 1837105152 | bytes 25165824 | tf_op jit(solution)/shard_map/dot_general | solution.py:70
  397.6 4.6 fusion.250
  402.3 4.6 fusion.249
  406.9 9.9 %multiply_convert_fusion = (bf16[1024,1536]{1,0:T(8,128)(2,1)S(1)}, bf16[1024,1536]{1,0:T(8,128)(2,1)}, bf16[1024,1536]{1,0:T(8,128)(2,1)}) fusion(f32[1024,1536]{1,0:T(8,128)} %fusion.249, f32[1024,1536]{1,0:T(8,128)} %fusion.250, bf16[1536,576]{1,0:T(8,128)(2,1)S(1)} %copy-done.56, bf16[2,1024,576]{1,2,0:T(8,128)(2,1)S(1)} %copy-done.53), kind=kOutput, calls=%fused_computation.72 | convolution fusion | flops 1837105152 | bytes 25165824 | tf_op jit(solution)/shard_map/dot_general | solution.py:70
  416.8 5.1 fusion.252
  427.7 9.8 %fusion.102 = f32[3,64,1024]{2,1,0:T(8,128)} fusion(f32[1,3,3,512,1024]{3,4,2,1,0:T(8,128)} %get-tuple-element.121, f32[3,3,512]{2,1,0:T(4,128)S(1)} %log_add_fusion, pred[512,1024]{0,1:T(8,128)(4,1)S(1)} %get-tuple-element.114, bf16[1,1024,3,3,64]{1,4,3,2,0:T(8,128)(2,1)S(1)} %bitcast.594), kind=kOutput, calls=%fused_computation.169 | convolution fusion | flops 618135552 | bytes 20799488 | tf_op jit(solution)/shard_map/nkgqs,nqkgd->nskd/dot_general | solution.py:130
  437.5 12.6 %fusion = (f32[3,3,512]{2,1,0:T(4,128)S(1)}, f32[3,1024,512,3]{2,1,3,0:T(8,128)}) fusion(f32[1,3,3,512,1024]{3,4,2,1,0:T(8,128)} %get-tuple-element.121, f32[3,3,512]{2,1,0:T(4,128)S(1)} %log_add_fusion, pred[512,1024]{0,1:T(8,128)(4,1)S(1)} %get-tuple-element.114, bf16[1024,3,64,1]{0,2,3,1:T(8,128)(2,1)S(1)} %bitcast.584, ...), kind=kOutput, calls=%fused_computation.6 | convolution fusion | flops 622849536 | bytes 39299072 | tf_op jit(solution)/shard_map/nqkgd,nskd->nkgqs/dot_general | solution.py:133
  450.1 12.7 %fusion.4 = (f32[3,3,512]{2,1,0:T(4,128)S(1)}, f32[3,1024,512,3]{2,1,3,0:T(8,128)}) fusion(f32[1,3,3,512,1024]{3,4,2,1,0:T(8,128)} %get-tuple-element.123, f32[3,3,512]{2,1,0:T(4,128)S(1)} %log_add_fusion.1, pred[512,1024]{0,1:T(8,128)(4,1)S(1)} %get-tuple-element.113, bf16[1024,3,64,1]{0,2,3,1:T(8,128)(2,1)S(1)} %bitcast.585, ...), kind=kOutput, calls=%fused_computation.12 | convolution fusion | flops 622849536 | bytes 39299072 | tf_op jit(solution)/shard_map/nqkgd,nskd->nkgqs/dot_general | solution.py:133
  462.9 13.8 %fusion.30 = bf16[3,3,512,1024]{2,3,1,0:T(8,128)(2,1)S(1)} fusion(f32[3,1024,512,3]{2,1,3,0:T(8,128)} %get-tuple-element.141, f32[1,3,3,512,1024]{3,4,2,1,0:T(8,128)} %get-tuple-element.123, f32[3,3,512]{2,1,0:T(4,128)S(1)} %get-tuple-element.140, f32[3,3,512]{2,1,0:T(4,128)S(1)} %log_add_fusion.1, pred[512,1024]{0,1:T(8,128)(4,1)S(1)} %get-tuple-element.113), kind=kLoop, calls=%fused_computation.54 | loop fusion | flops 28311552 | bytes 47747072 | tf_op jit(solution)/shard_map/reshape.214
  484.5 9.4 fusion.108
  493.9 13.4 %fusion.8 = (f32[3,3,512]{2,1,0:T(4,128)}, f32[3,1024,512,3]{2,1,3,0:T(8,128)}) fusion(f32[1,3,3,512,1024]{3,4,2,1,0:T(8,128)} %get-tuple-element.125, f32[3,3,512]{2,1,0:T(4,128)S(1)} %log_add_fusion.2, pred[512,1024]{0,1:T(8,128)(4,1)S(1)} %copy-done.12, bf16[1024,3,64,1]{0,2,3,1:T(8,128)(2,1)S(1)} %bitcast.580, bf16[1,1024,3,3,64]{1,4,3,2,0:T(8,128)(2,1)S(1)} %bitcast.599), kind=kOutput, calls=%fused_computation.18 | convolution fusion | flops 622849536 | bytes 39299072 | tf_op jit(solution)/shard_map/nqkgd,nskd->nkgqs/dot_general | solution.py:133
  507.3 12.5 %fusion.12 = (f32[3,3,512]{2,1,0:T(4,128)S(1)}, f32[3,1024,512,3]{2,1,3,0:T(8,128)}) fusion(f32[1,3,3,512,1024]{3,4,2,1,0:T(8,128)} %get-tuple-element.127, f32[3,3,512]{2,1,0:T(4,128)S(1)} %log_add_fusion.3, pred[512,1024]{0,1:T(8,128)(4,1)S(1)} %copy-done.14, bf16[1024,3,64,1]{0,2,3,1:T(8,128)(2,1)S(1)} %bitcast.581, ...), kind=kOutput, calls=%fused_computation.24 | convolution fusion | flops 622849536 | bytes 39299072 | tf_op jit(solution)/shard_map/nqkgd,nskd->nkgqs/dot_general | solution.py:133
  519.8 14.2 %fusion.28 = bf16[3,3,512,1024]{2,3,1,0:T(8,128)(2,1)S(1)} fusion(f32[3,1024,512,3]{2,1,3,0:T(8,128)} %get-tuple-element.137, f32[1,3,3,512,1024]{3,4,2,1,0:T(8,128)} %get-tuple-element.127, f32[3,3,512]{2,1,0:T(4,128)S(1)} %get-tuple-element.136, f32[3,3,512]{2,1,0:T(4,128)S(1)} %log_add_fusion.3, pred[512,1024]{0,1:T(8,128)(4,1)S(1)} %copy-done.14), kind=kLoop, calls=%fused_computation.52 | loop fusion | flops 28311552 | bytes 47747072 | tf_op jit(solution)/shard_map/reshape.154
  552.2 4.6 reshape.1665
  556.7 4.7 reshape.1666
  566.9 7.2 convolution_add_fusion
  574.1 5.3 copy.110
  579.4 5.4 reshape.1667
  584.8 8.7 fusion.120
  593.6 8.3 fusion.123
  609.1 19.3 %fusion.31 = bf16[3,3,512,1024]{2,3,1,0:T(8,128)(2,1)} fusion(f32[3,1024,512,3]{2,1,3,0:T(8,128)} %get-tuple-element.139, f32[1,3,3,512,1024]{3,4,2,1,0:T(8,128)} %get-tuple-element.121, f32[3,3,512]{2,1,0:T(4,128)S(1)} %get-tuple-element.138, f32[3,3,512]{2,1,0:T(4,128)S(1)} %log_add_fusion, pred[512,1024]{0,1:T(8,128)(4,1)S(1)} %get-tuple-element.114), kind=kLoop, calls=%fused_computation.55 | loop fusion | flops 28311552 | bytes 47747072 | tf_op jit(solution)/shard_map/reshape.222
  628.4 6.6 convolution_bitcast_fusion.2
  635.0 7.8 fusion.99
  647.9 14.0 %fusion.29 = bf16[3,3,512,1024]{2,3,1,0:T(8,128)(2,1)} fusion(f32[3,1024,512,3]{2,1,3,0:T(8,128)} %get-tuple-element.135, f32[1,3,3,512,1024]{3,4,2,1,0:T(8,128)S(1)} %bitcast.555, f32[3,3,512]{2,1,0:T(4,128)S(1)} %copy-done.135, f32[3,3,512]{2,1,0:T(4,128)S(1)} %copy-done.115, pred[512,1024]{0,1:T(8,128)(4,1)S(1)} %copy-done.12), kind=kLoop, calls=%fused_computation.53 | loop fusion | flops 28311552 | bytes 47747072 | tf_op jit(solution)/shard_map/reshape.162
  661.9 5.5 convolution_bitcast_fusion.4
  698.0 38.9 %psum.7 = f32[2,576]{1,0:T(2,128)S(1)} all-reduce(f32[2,576]{1,0:T(2,128)S(1)} %maximum_add_fusion), channel_id=1, replica_groups=mesh['dp'=32] {'dp'}, use_global_device_ids=true, to_apply=%region_35.36 | all-reduce | flops 1152 | bytes 9216 | tf_op jit(solution)/shard_map/psum | solution.py:387
  737.0 4.7 fusion.84
  752.4 186.7 %all-reduce.10.cloned.1.call-done = (f32[331776]{0:T(1024)}, f32[110592]{0:T(1024)}, f32[110592]{0:T(1024)}, f32[331776]{0:T(1024)}, f32[884736]{0:T(1024)}, /*index=5*/f32[884736]{0:T(1024)}, f32[884736]{0:T(1024)}) async-done(((f32[331776]{0:T(1024)}, f32[110592]{0:T(1024)}, f32[110592]{0:T(1024)}, f32[331776]{0:T(1024)}, f32[884736]{0:T(1024)}, /*index=5*/f32[884736]{0:T(1024)}, f32[884736]{0:T(1024)}), ...) | async-done | bytes 14155792
  (501 shorter events, 173.1 us)
Async XLA Ops:
  7.2 341.3 %all-gather.8.cloned.1.call-start = ((), (), s32[]{:S(2)}) async-start(), calls=%async_computation | async-start | bytes 1824768 | tf_op jit(solution)/shard_map/all_gather | solution.py:350
  8.8 57.8 %copy-start.18 = (bf16[2,1024,576]{1,2,0:T(8,128)(2,1)S(1)}, bf16[2,1024,576]{1,2,0:T(8,128)(2,1)}, u32[]{:S(2)}) copy-start(bf16[2,1024,576]{1,2,0:T(8,128)(2,1)} %param.27) | copy-start | bytes 7077892
  8.8 344.2 %all-gather.10.cloned.1.call-start = ((), (), s32[]{:S(2)}) async-start(), calls=%async_computation.1 | async-start | bytes 1824768 | tf_op jit(solution)/shard_map/all_gather | solution.py:351
  10.6 358.8 %all-gather.12.cloned.1.call-start = ((), (), s32[]{:S(2)}) async-start(), calls=%async_computation.2 | async-start | bytes 1824768 | tf_op jit(solution)/shard_map/all_gather | solution.py:352
  12.2 927.0 %all-reduce.10.cloned.1.call-start = ((), (), s32[]{:S(2)}) async-start(), calls=%async_computation.3 | async-start | bytes 28311552
  17.6 152.2 %copy-start.146 = (f32[576]{0:T(1024)}, f32[576]{0:T(1024)S(1)}, u32[]{:S(2)}) copy-start(f32[576]{0:T(1024)S(1)} %get-tuple-element.39) | copy-start | bytes 6916
  19.8 150.0 %copy-start.148 = (f32[1024]{0:T(1024)}, f32[1024]{0:T(1024)S(1)}, u32[]{:S(2)}) copy-start(f32[1024]{0:T(1024)S(1)} %fusion.199) | copy-start | bytes 12292
  20.3 145.7 %copy-start.150 = (f32[1024]{0:T(1024)}, f32[1024]{0:T(1024)S(1)}, u32[]{:S(2)}) copy-start(f32[1024]{0:T(1024)S(1)} %fusion.201) | copy-start | bytes 12292
  172.4 50.4 %copy-start.159 = (s32[1024]{0:T(1024)}, s32[1024]{0:T(1024)S(1)}, u32[]{:S(2)}) copy-start(s32[1024]{0:T(1024)S(1)} %iota.88) | copy-start | bytes 12292
  231.3 25.9 %copy-start.11 = (pred[512,1024]{0,1:T(8,128)(4,1)}, pred[512,1024]{0,1:T(8,128)(4,1)S(1)}, u32[]{:S(2)}) copy-start(pred[512,1024]{0,1:T(8,128)(4,1)S(1)} %get-tuple-element.115) | copy-start | bytes 1572868
  231.3 45.7 %copy-start.13 = (pred[512,1024]{0,1:T(8,128)(4,1)}, pred[512,1024]{0,1:T(8,128)(4,1)S(1)}, u32[]{:S(2)}) copy-start(pred[512,1024]{0,1:T(8,128)(4,1)S(1)} %get-tuple-element.116) | copy-start | bytes 1572868
  231.3 231.5 %copy-start.16 = (pred[512,1024]{0,1:T(8,128)(4,1)}, pred[512,1024]{0,1:T(8,128)(4,1)S(1)}, u32[]{:S(2)}) copy-start(pred[512,1024]{0,1:T(8,128)(4,1)S(1)} %get-tuple-element.113) | copy-start | bytes 1572868
  303.2 28.4 %copy-start.129 = (f32[3,3,512]{2,1,0:T(4,128)}, f32[3,3,512]{2,1,0:T(4,128)S(1)}, u32[]{:S(2)}) copy-start(f32[3,3,512]{2,1,0:T(4,128)S(1)} %get-tuple-element.122) | copy-start | bytes 55300
  321.8 20.2 %copy-start.105 = (bf16[3,64,3,512]{3,1,2,0:T(8,128)(2,1)}, bf16[3,64,3,512]{3,1,2,0:T(8,128)(2,1)S(1)}, u32[]{:S(2)}) copy-start(bf16[3,64,3,512]{3,1,2,0:T(8,128)(2,1)S(1)} %fusion.95) | copy-start | bytes 1769476
  344.4 80.5 %copy-start.1 = (f32[1024,576]{0,1:T(8,128)}, f32[1024,576]{0,1:T(8,128)S(1)}, u32[]{:S(2)}) copy-start(f32[1024,576]{0,1:T(8,128)S(1)} %get-tuple-element.129) | copy-start | bytes 7077892
  347.1 146.8 %copy-start.114 = (f32[3,3,512]{2,1,0:T(4,128)}, f32[3,3,512]{2,1,0:T(4,128)S(1)}, u32[]{:S(2)}) copy-start(f32[3,3,512]{2,1,0:T(4,128)S(1)} %log_add_fusion.2) | copy-start | bytes 55300
  426.5 56.9 %copy-start.3 = (f32[1024,576]{0,1:T(8,128)}, f32[1024,576]{0,1:T(8,128)S(1)}, u32[]{:S(2)}) copy-start(f32[1024,576]{0,1:T(8,128)S(1)} %get-tuple-element.86) | copy-start | bytes 7077892
  427.6 22.5 %copy-start.91 = (bf16[1024,576]{0,1:T(8,128)(2,1)}, bf16[1024,576]{0,1:T(8,128)(2,1)S(1)}, u32[]{:S(2)}) copy-start(bf16[1024,576]{0,1:T(8,128)(2,1)S(1)} %convolution_convert_fusion) | copy-start | bytes 3538948
  484.5 22.8 %copy-start.93 = (bf16[1024,576]{0,1:T(8,128)(2,1)}, bf16[1024,576]{0,1:T(8,128)(2,1)S(1)}, u32[]{:S(2)}) copy-start(bf16[1024,576]{0,1:T(8,128)(2,1)S(1)} %convolution_convert_fusion.1) | copy-start | bytes 3538948
  609.1 19.3 %copy-start.70 = (bf16[1024,3,32]{0,2,1:T(8,128)(2,1)S(1)}, bf16[1024,3,32]{0,2,1:T(8,128)(2,1)}, u32[]{:S(2)}) copy-start(bf16[1024,3,32]{0,2,1:T(8,128)(2,1)} %get-tuple-element.94) | copy-start | bytes 589828
  609.1 19.3 %copy-start.73 = (bf16[1024,3,32]{0,2,1:T(8,128)(2,1)S(1)}, bf16[1024,3,32]{0,2,1:T(8,128)(2,1)}, u32[]{:S(2)}) copy-start(bf16[1024,3,32]{0,2,1:T(8,128)(2,1)} %get-tuple-element.95) | copy-start | bytes 589828
  609.1 38.7 %slice-start = ((s8[18874368]{0:T(1024)(128)(4,1)}), s8[4194304]{0:T(1024)(128)(4,1)S(1)}, s32[]{:S(2)}) async-start(s8[18874368]{0:T(1024)(128)(4,1)} %bitcast.554), calls=%async_computation.4 | async-start | bytes 8388608
  609.1 38.7 %slice-start.1 = ((s8[18874368]{0:T(1024)(128)(4,1)}), s8[4194304]{0:T(1024)(128)(4,1)S(1)}, s32[]{:S(2)}) async-start(s8[18874368]{0:T(1024)(128)(4,1)} %bitcast.554), calls=%async_computation.5 | async-start | bytes 8388608
  609.1 38.7 %slice-start.2 = ((s8[18874368]{0:T(1024)(128)(4,1)}), s8[4194304]{0:T(1024)(128)(4,1)S(1)}, s32[]{:S(2)}) async-start(s8[18874368]{0:T(1024)(128)(4,1)} %bitcast.554), calls=%async_computation.6 | async-start | bytes 8388608
  628.4 19.4 %slice-start.3 = ((s8[18874368]{0:T(1024)(128)(4,1)}), s8[4194304]{0:T(1024)(128)(4,1)S(1)}, s32[]{:S(2)}) async-start(s8[18874368]{0:T(1024)(128)(4,1)} %bitcast.554), calls=%async_computation.7 | async-start | bytes 8388608
  647.8 19.7 %copy-start.47 = (f32[3,64,1024]{2,1,0:T(8,128)S(1)}, f32[3,64,1024]{2,1,0:T(8,128)}, u32[]{:S(2)}) copy-start(f32[3,64,1024]{2,1,0:T(8,128)} %convolution_bitcast_fusion.11) | copy-start | bytes 2359300
  695.3 41.6 %copy-start.2 = (f32[1024,576]{0,1:T(8,128)S(1)}, f32[1024,576]{0,1:T(8,128)}, u32[]{:S(2)}) copy-start(f32[1024,576]{0,1:T(8,128)} %copy-done.1) | copy-start | bytes 7077892
  749.7 189.5 %copy-start.109 = (f32[27648]{0:T(1024)S(1)}, f32[27648]{0:T(1024)}, u32[]{:S(2)}) copy-start(f32[27648]{0:T(1024)} %param.35) | copy-start | bytes 331780
  749.7 189.5 %copy-start.124 = (f32[27648]{0:T(1024)S(1)}, f32[27648]{0:T(1024)}, u32[]{:S(2)}) copy-start(f32[27648]{0:T(1024)} %param.42) | copy-start | bytes 331780
  749.7 189.5 %copy-start.125 = (f32[27648]{0:T(1024)S(1)}, f32[27648]{0:T(1024)}, u32[]{:S(2)}) copy-start(f32[27648]{0:T(1024)} %param.49) | copy-start | bytes 331780
  749.7 191.1 %copy-start.107 = (f32[27648]{0:T(1024)S(1)}, f32[27648]{0:T(1024)}, u32[]{:S(2)}) copy-start(f32[27648]{0:T(1024)} %param.36) | copy-start | bytes 331780
  749.7 191.1 %copy-start.108 = (f32[27648]{0:T(1024)S(1)}, f32[27648]{0:T(1024)}, u32[]{:S(2)}) copy-start(f32[27648]{0:T(1024)} %param.37) | copy-start | bytes 331780
  749.7 191.1 %copy-start.120 = (f32[27648]{0:T(1024)S(1)}, f32[27648]{0:T(1024)}, u32[]{:S(2)}) copy-start(f32[27648]{0:T(1024)} %param.44) | copy-start | bytes 331780
  749.7 191.1 %copy-start.121 = (f32[27648]{0:T(1024)S(1)}, f32[27648]{0:T(1024)}, u32[]{:S(2)}) copy-start(f32[27648]{0:T(1024)} %param.51) | copy-start | bytes 331780
  749.8 191.1 %copy-start.122 = (f32[27648]{0:T(1024)S(1)}, f32[27648]{0:T(1024)}, u32[]{:S(2)}) copy-start(f32[27648]{0:T(1024)} %param.50) | copy-start | bytes 331780
  749.8 191.1 %copy-start.123 = (f32[27648]{0:T(1024)S(1)}, f32[27648]{0:T(1024)}, u32[]{:S(2)}) copy-start(f32[27648]{0:T(1024)} %param.43) | copy-start | bytes 331780
  752.3 190.4 %copy-start.117 = (f32[10368]{0:T(1024)S(1)}, f32[10368]{0:T(1024)}, u32[]{:S(2)}) copy-start(f32[10368]{0:T(1024)} %param.34) | copy-start | bytes 124420
  752.3 190.4 %copy-start.119 = (f32[10368]{0:T(1024)S(1)}, f32[10368]{0:T(1024)}, u32[]{:S(2)}) copy-start(f32[10368]{0:T(1024)} %param.31) | copy-start | bytes 124420
  752.3 190.4 %copy-start.138 = (f32[10368]{0:T(1024)S(1)}, f32[10368]{0:T(1024)}, u32[]{:S(2)}) copy-start(f32[10368]{0:T(1024)} %param.41) | copy-start | bytes 124420
  752.3 190.4 %copy-start.139 = (f32[10368]{0:T(1024)S(1)}, f32[10368]{0:T(1024)}, u32[]{:S(2)}) copy-start(f32[10368]{0:T(1024)} %param.48) | copy-start | bytes 124420
  752.4 190.4 %copy-start.140 = (f32[10368]{0:T(1024)S(1)}, f32[10368]{0:T(1024)}, u32[]{:S(2)}) copy-start(f32[10368]{0:T(1024)} %param.45) | copy-start | bytes 124420
  752.4 190.4 %copy-start.141 = (f32[10368]{0:T(1024)S(1)}, f32[10368]{0:T(1024)}, u32[]{:S(2)}) copy-start(f32[10368]{0:T(1024)} %param.38) | copy-start | bytes 124420
  752.4 192.0 %copy-start.136 = (f32[3456]{0:T(1024)S(1)}, f32[3456]{0:T(1024)}, u32[]{:S(2)}) copy-start(f32[3456]{0:T(1024)} %param.33) | copy-start | bytes 41476
  752.4 192.0 %copy-start.137 = (f32[3456]{0:T(1024)S(1)}, f32[3456]{0:T(1024)}, u32[]{:S(2)}) copy-start(f32[3456]{0:T(1024)} %param.32) | copy-start | bytes 41476
  752.4 192.0 %copy-start.154 = (f32[3456]{0:T(1024)S(1)}, f32[3456]{0:T(1024)}, u32[]{:S(2)}) copy-start(f32[3456]{0:T(1024)} %param.40) | copy-start | bytes 41476
  752.4 192.0 %copy-start.155 = (f32[3456]{0:T(1024)S(1)}, f32[3456]{0:T(1024)}, u32[]{:S(2)}) copy-start(f32[3456]{0:T(1024)} %param.47) | copy-start | bytes 41476
  752.4 192.0 %copy-start.156 = (f32[3456]{0:T(1024)S(1)}, f32[3456]{0:T(1024)}, u32[]{:S(2)}) copy-start(f32[3456]{0:T(1024)} %param.46) | copy-start | bytes 41476
  752.4 192.0 %copy-start.157 = (f32[3456]{0:T(1024)S(1)}, f32[3456]{0:T(1024)}, u32[]{:S(2)}) copy-start(f32[3456]{0:T(1024)} %param.39) | copy-start | bytes 41476
  (133 other events, 697.9 us)
Sparse Core Ops, SparseCore 0:
  11.4 58.9 all-gather.7
  73.9 56.1 all-gather.9
  133.5 55.2 all-gather.11
  688.2 250.9 all-reduce.9
where the time goes:
time: 961 us; the launch traced here: 953 us
  matrix products  318 us (33%)
  blocking collectives  209 us (22%)
  waiting for transfers between devices  187 us (19%)
  other arithmetic  158 us (16%)
  local copies, waits for them, and re-layouts  64.1 us (7%)
  between operations  16.3 us (2%)
    unnamed x5, waiting for transfers between devices  187 us
    another operation x14, other arithmetic  70.4 us
    dot_general x4, matrix products, attention_backward(): jnp.einsum('nqkgd,nskd->nkgqs', back_block, value_rows, preferred_element...  51.2 us
    all_gather x1, blocking collectives, body(): lax.all_gather(low_shards[0], 'dp', axis=0, tiled=True)  44.7 us
    all_gather x1, blocking collectives, body(): lax.all_gather(low_shards[2], 'dp', axis=0, tiled=True)  44.7 us
    dot_general x14, matrix products, matmul(): return jnp.dot(left, right, preferred_element_type=jnp.float32)  43.8 us
    all_gather x1, blocking collectives, body(): lax.all_gather(low_shards[3], 'dp', axis=0, tiled=True)  42.9 us
    dot_general x14, matrix products, right_dot(): lax.dot_general(left, right, (((1,), (1,)), ((), ())), preferred_element_...  42.9 us
  transfers between devices with their start and end apart: 4, of which 1 were waited for; matrix products, arithmetic and copies ran while one was open for 22% of the time, Pallas kernels for 0%

commit v1 on v0

v1 whole, which is shorter than its diff:
```python
import functools

import jax
import jax.numpy as jnp
from jax import lax
from jax.experimental import pallas as pl
from jax.experimental.pallas import tpu as pltpu
from jax.sharding import PartitionSpec as P

D = 576
HEADS = 9
KV_HEADS = 3
HEAD = 64
FF = 1536
STEP = 10
BLOCK = 256
VMEM_LIMIT = 58 * 2**20

norm_eps = 1e-05
rope_base = 100000.0
learn_rate = 0.06
gain_rate = 0.4
beta_first = 0.9
beta_second = 0.95
adam_eps = 1e-08
decay_rate = 0.1


def doc_positions(segments):
    places = jnp.arange(segments.shape[-1], dtype=jnp.int32)
    first_col = jnp.ones(segments.shape[:-1] + (1,), dtype=jnp.bool_)
    change = jnp.concatenate([first_col, segments[..., 1:] != segments[..., :-1]], axis=-1)
    starts = lax.cummax(jnp.where(change, places, jnp.zeros_like(places)), axis=segments.ndim - 1)
    return places - starts


def rope_tables(positions):
    half_size = HEAD // 2
    frequency = rope_base ** (-(jnp.arange(half_size, dtype=jnp.float32) * 2.0 / HEAD))
    angles = positions.astype(jnp.float32)[..., None] * frequency
    cosine, sine = jnp.cos(angles), jnp.sin(angles)
    return (
        jnp.concatenate([cosine, cosine], axis=-1),
        jnp.concatenate([-sine, sine], axis=-1),
    )


def dot(left, right, left_dim=1, right_dim=0):
    return lax.dot_general(
        left,
        right,
        (((left_dim,), (right_dim,)), ((), ())),
        preferred_element_type=jnp.float32,
    )


def swap_halves(values):
    half = HEAD // 2
    return jnp.concatenate([values[:, half:], values[:, :half]], axis=1)


def norm_parts(values):
    scale = lax.rsqrt(jnp.mean(values * values, axis=-1, keepdims=True) + norm_eps)
    return scale, values * scale


def norm_back(scale, unit, gain, upstream):
    weighted = gain * upstream
    return scale * (weighted - unit * jnp.mean(weighted * unit, axis=-1, keepdims=True))


def mask_block(bias, seg_col, seg_row, start, length):
    key_seg = seg_col[0, 0:length, :]
    query_seg = seg_row[0, :, start : start + BLOCK]
    key_place = lax.broadcasted_iota(jnp.int32, (length, BLOCK), 0)
    query_place = lax.broadcasted_iota(jnp.int32, (length, BLOCK), 1) + start
    allowed = jnp.logical_and(key_seg == query_seg, key_place <= query_place)
    bias[0:length, :] = jnp.where(allowed, 0.0, -1e30)


def attend_kernel(
    x, gains, seg_col, seg_row, cosine, sine, wq, wk, wv, q_out, k_out, v_out, lse_out, att_out,
    att, bias
):
    seq = x.shape[1]
    _, unit = norm_parts(x[0].astype(jnp.float32))
    normed = (unit * gains[0:1, :]).astype(jnp.bfloat16)
    cos, sin = cosine[0], sine[0]
    q_lin = dot(normed, wq[...])
    for h in range(HEADS):
        part = q_lin[:, h * HEAD : (h + 1) * HEAD]
        turned = (part * cos + swap_halves(part) * sin).astype(jnp.bfloat16)
        q_out[0, h] = turned * jnp.bfloat16(0.125)
    k_lin = dot(normed, wk[...])
    v_lin = dot(normed, wv[...])
    for j in range(KV_HEADS):
        part = k_lin[:, j * HEAD : (j + 1) * HEAD]
        k_out[0, j] = (part * cos + swap_halves(part) * sin).astype(jnp.bfloat16)
        v_out[0, j] = v_lin[:, j * HEAD : (j + 1) * HEAD].astype(jnp.bfloat16)
    for start in range(0, seq, BLOCK):
        length = start + BLOCK
        mask_block(bias, seg_col, seg_row, start, length)

        def head_step(h, carry):
            j = lax.div(h, HEADS // KV_HEADS)
            keys = k_out[0, j, 0:length, :]
            values = v_out[0, j, 0:length, :]
            queries = q_out[0, h, start : start + BLOCK, :]
            scores = dot(keys, queries, 1, 1) + bias[0:length, :]
            top = jnp.max(scores, axis=0, keepdims=True)
            terms = jnp.exp(scores - top)
            total = jnp.sum(terms, axis=0, keepdims=True)
            probs = (terms * (1.0 / total)).astype(jnp.bfloat16)
            lse_out[0, h, :, start : start + BLOCK] = top + jnp.log(total)
            att[h, start : start + BLOCK, :] = dot(probs, values, 0, 0).astype(jnp.bfloat16)
            return carry

        lax.fori_loop(0, HEADS, head_step, 0)
    att_out[0] = jnp.concatenate([att[h] for h in range(HEADS)], axis=1)


def feed_kernel(
    x, att, cot, gains, wo, wg, wu, wd,
    out, mid_back, att_back, do_out, dg_out, du_out, dd_out, gain_out,
    acc_o, acc_g, acc_u, acc_d
):
    step = pl.program_id(0)

    @pl.when(step == 0)
    def _():
        for ref in (acc_o, acc_g, acc_u, acc_d, gain_out):
            ref[...] = jnp.zeros_like(ref)

    gain = gains[1:2, :]
    middle = x[...].astype(jnp.float32) + dot(att[...], wo[...])
    scale, unit = norm_parts(middle)
    normed = (unit * gain).astype(jnp.bfloat16)
    gate = dot(normed, wg[...])
    up = dot(normed, wu[...])
    sig = 1.0 / (1.0 + jnp.exp(-gate))
    sil = gate * sig
    hidden = (sil * up).astype(jnp.bfloat16)
    out[...] = (middle + dot(hidden, wd[...])).astype(jnp.bfloat16)
    back = cot[...]
    acc_d[...] += dot(hidden, back, 0, 0)
    hidden_back = dot(back, wd[...], 1, 1)
    gate_back = (hidden_back * up * sig * (1.0 + gate * (1.0 - sig))).astype(jnp.bfloat16)
    up_back = (hidden_back * sil).astype(jnp.bfloat16)
    acc_g[...] += dot(normed, gate_back, 0, 0)
    acc_u[...] += dot(normed, up_back, 0, 0)
    upstream = dot(gate_back, wg[...], 1, 1) + dot(up_back, wu[...], 1, 1)
    gain_out[...] += jnp.sum(upstream * unit, axis=0, keepdims=True)
    middle_back = back.astype(jnp.float32) + norm_back(scale, unit, gain, upstream)
    mid_back[...] = middle_back
    branch = middle_back.astype(jnp.bfloat16)
    acc_o[...] += dot(att[...], branch, 0, 0)
    att_back[...] = dot(branch, wo[...], 1, 1).astype(jnp.bfloat16)

    @pl.when(step == pl.num_programs(0) - 1)
    def _():
        for ref, acc in ((do_out, acc_o), (dg_out, acc_g), (du_out, acc_u), (dd_out, acc_d)):
            ref[...] = acc[...].astype(jnp.bfloat16)


def attend_back_kernel(
    x, gains, seg_col, seg_row, cosine, sine, wq, wk, wv, q_in, k_in, v_in, lse, att_back, mid_back,
    x_back, dq_out, dk_out, dv_out, gain_out,
    ob, dq, dk, dv, bias, acc_q, acc_k, acc_v
):
    step = pl.program_id(0)
    seq = x.shape[1]

    @pl.when(step == 0)
    def _():
        for ref in (acc_q, acc_k, acc_v, gain_out):
            ref[...] = jnp.zeros_like(ref)

    dk[...] = jnp.zeros_like(dk)
    dv[...] = jnp.zeros_like(dv)
    for h in range(HEADS):
        ob[h] = att_back[0, :, h * HEAD : (h + 1) * HEAD]
    for start in range(0, seq, BLOCK):
        length = start + BLOCK
        mask_block(bias, seg_col, seg_row, start, length)

        def head_step(h, carry):
            j = lax.div(h, HEADS // KV_HEADS)
            keys = k_in[0, j, 0:length, :]
            values = v_in[0, j, 0:length, :]
            queries = q_in[0, h, start : start + BLOCK, :]
            out_back = ob[h, start : start + BLOCK, :]
            scores = dot(keys, queries, 1, 1) + bias[0:length, :]
            probs = jnp.exp(scores - lse[0, h, :, start : start + BLOCK])
            dv[j, 0:length, :] += dot(probs.astype(jnp.bfloat16), out_back)
            weighted = probs * dot(values, out_back, 1, 1)
            delta = jnp.sum(weighted, axis=0, keepdims=True)
            score_back = (weighted - probs * delta).astype(jnp.bfloat16)
            dk[j, 0:length, :] += dot(score_back, queries)
            dq[h, start : start + BLOCK, :] = dot(score_back, keys, 0, 0) * 0.125
            return carry

        lax.fori_loop(0, HEADS, head_step, 0)

    cos, sin = cosine[0], sine[0]

    def turn_back(part):
        return (part * cos - swap_halves(part) * sin).astype(jnp.bfloat16)

    q_back = jnp.concatenate([turn_back(dq[h]) for h in range(HEADS)], axis=1)
    k_back = jnp.concatenate([turn_back(dk[j]) for j in range(KV_HEADS)], axis=1)
    v_back = jnp.concatenate([dv[j].astype(jnp.bfloat16) for j in range(KV_HEADS)], axis=1)
    gain = gains[0:1, :]
    scale, unit = norm_parts(x[0].astype(jnp.float32))
    normed = (unit * gain).astype(jnp.bfloat16)
    acc_q[...] += dot(normed, q_back, 0, 0)
    acc_k[...] += dot(normed, k_back, 0, 0)
    acc_v[...] += dot(normed, v_back, 0, 0)
    upstream = (
        dot(q_back, wq[...], 1, 1) + dot(k_back, wk[...], 1, 1) + dot(v_back, wv[...], 1, 1)
    )
    gain_out[...] += jnp.sum(upstream * unit, axis=0, keepdims=True)
    x_back[0] = mid_back[0] + norm_back(scale, unit, gain, upstream)

    @pl.when(step == pl.num_programs(0) - 1)
    def _():
        for ref, acc in ((dq_out, acc_q), (dk_out, acc_k), (dv_out, acc_v)):
            ref[...] = acc[...].astype(jnp.bfloat16)


def whole(shape):
    return pl.BlockSpec(shape, lambda i: (0,) * len(shape))


def per_step(shape):
    return pl.BlockSpec((1,) + shape[1:], lambda i: (i,) + (0,) * (len(shape) - 1))


def sds(shape, dtype):
    return jax.ShapeDtypeStruct(shape, dtype)


def params():
    return pltpu.CompilerParams(
        dimension_semantics=("arbitrary",), vmem_limit_bytes=VMEM_LIMIT
    )


def attention_forward(x, gains, seg_col, seg_row, cosine, sine, wq, wk, wv):
    seqs, seq = x.shape[0], x.shape[1]
    outs = [
        ((seqs, HEADS, seq, HEAD), jnp.bfloat16),
        ((seqs, KV_HEADS, seq, HEAD), jnp.bfloat16),
        ((seqs, KV_HEADS, seq, HEAD), jnp.bfloat16),
        ((seqs, HEADS, 1, seq), jnp.float32),
        ((seqs, seq, D), jnp.bfloat16),
    ]
    return pl.pallas_call(
        attend_kernel,
        grid=(seqs,),
        out_shape=[sds(*o) for o in outs],
        in_specs=[per_step(x.shape), whole(gains.shape)]
        + [per_step(a.shape) for a in (seg_col, seg_row, cosine, sine)]
        + [whole(w.shape) for w in (wq, wk, wv)],
        out_specs=[per_step(o[0]) for o in outs],
        scratch_shapes=[
            pltpu.VMEM((HEADS, seq, HEAD), jnp.bfloat16),
            pltpu.VMEM((seq, BLOCK), jnp.float32),
        ],
        compiler_params=params(),
        cost_estimate=pl.CostEstimate(
            flops=60 * 10**9, bytes_accessed=20 * 10**6, transcendentals=2 * 10**7
        ),
        name="attention_forward",
    )(x, gains, seg_col, seg_row, cosine, sine, wq, wk, wv)


def feed_forward(x, att, cot, gains, wo, wg, wu, wd):
    tokens = x.shape[0]
    rows = pl.BlockSpec((BLOCK, D), lambda i: (i, 0))
    fixed = lambda shape: pl.BlockSpec(shape, lambda i: (0, 0), pipeline_mode=pl.Buffered(1))
    weights = (wo, wg, wu, wd)
    return pl.pallas_call(
        feed_kernel,
        grid=(tokens // BLOCK,),
        out_shape=[
            sds((tokens, D), jnp.bfloat16),
            sds((tokens, D), jnp.float32),
            sds((tokens, D), jnp.bfloat16),
        ]
        + [sds(w.shape, jnp.bfloat16) for w in weights]
        + [sds((1, D), jnp.float32)],
        in_specs=[rows, rows, rows, whole(gains.shape)] + [fixed(w.shape) for w in weights],
        out_specs=[rows, rows, rows] + [fixed(w.shape) for w in weights] + [whole((1, D))],
        scratch_shapes=[pltpu.VMEM(w.shape, jnp.float32) for w in weights],
        compiler_params=params(),
        cost_estimate=pl.CostEstimate(
            flops=60 * 10**9, bytes_accessed=30 * 10**6, transcendentals=3 * 10**6
        ),
        name="feed_forward",
    )(x, att, cot, gains, wo, wg, wu, wd)


def attention_backward(
    x, gains, seg_col, seg_row, cosine, sine, wq, wk, wv, q, k, v, lse, att_back, mid_back
):
    seqs, seq = x.shape[0], x.shape[1]
    return pl.pallas_call(
        attend_back_kernel,
        grid=(seqs,),
        out_shape=[sds(x.shape, jnp.float32)]
        + [sds(w.shape, jnp.bfloat16) for w in (wq, wk, wv)]
        + [sds((1, D), jnp.float32)],
        in_specs=[per_step(x.shape), whole(gains.shape)]
        + [per_step(a.shape) for a in (seg_col, seg_row, cosine, sine)]
        + [whole(w.shape) for w in (wq, wk, wv)]
        + [per_step(a.shape) for a in (q, k, v, lse, att_back, mid_back)],
        out_specs=[per_step(x.shape)] + [whole(w.shape) for w in (wq, wk, wv)] + [whole((1, D))],
        scratch_shapes=[
            pltpu.VMEM((HEADS, seq, HEAD), jnp.bfloat16),
            pltpu.VMEM((HEADS, seq, HEAD), jnp.float32),
            pltpu.VMEM((KV_HEADS, seq, HEAD), jnp.float32),
            pltpu.VMEM((KV_HEADS, seq, HEAD), jnp.float32),
            pltpu.VMEM((seq, BLOCK), jnp.float32),
        ]
        + [pltpu.VMEM(w.shape, jnp.float32) for w in (wq, wk, wv)],
        compiler_params=params(),
        cost_estimate=pl.CostEstimate(
            flops=120 * 10**9, bytes_accessed=40 * 10**6, transcendentals=2 * 10**7
        ),
        name="attention_backward",
    )(x, gains, seg_col, seg_row, cosine, sine, wq, wk, wv, q, k, v, lse, att_back, mid_back)


def gather_group(shards, shapes, count):
    packed = jnp.concatenate([shard.astype(jnp.bfloat16) for shard in shards])
    rows = lax.all_gather(packed, "dp", axis=0, tiled=False)
    result = []
    place = 0
    for shard, shape in zip(shards, shapes):
        size = shard.shape[0]
        result.append(rows[:, place : place + size].reshape(shape))
        place += size
    return result


def reduce_group(grads, sizes, count):
    total = sum(sizes)
    lanes = -(-total // 128)
    parts = [grad.reshape(count, size) for grad, size in zip(grads, sizes)]
    if lanes * 128 > total:
        parts.append(jnp.zeros((count, lanes * 128 - total), jnp.bfloat16))
    held = jnp.concatenate(parts, axis=1).reshape(count, lanes, 128)
    me = lax.axis_index("dp")
    bit = 1
    while bit < count:
        pairs = held.reshape(held.shape[0] // 2, 2, lanes, 128)
        mine = lax.rem(lax.div(me, bit), 2)
        keep = lax.dynamic_index_in_dim(pairs, mine, 1, keepdims=False)
        give = lax.dynamic_index_in_dim(pairs, 1 - mine, 1, keepdims=False)
        got = lax.ppermute(give, "dp", [(d, d ^ bit) for d in range(count)])
        held = keep.astype(jnp.float32) + got.astype(jnp.float32)
        bit *= 2
        if bit < count:
            held = held.astype(jnp.bfloat16)
    flat = held.reshape(-1)
    result = []
    place = 0
    for size in sizes:
        result.append(flat[place : place + size])
        place += size
    return result


def butterfly(values, count):
    bit = 1
    while bit < count:
        values = values + lax.ppermute(values, "dp", [(d, d ^ bit) for d in range(count)])
        bit *= 2
    return values


def adam_step(weight_now, gradient, moment_one, moment_two, step_rate, decay_value):
    one_new = beta_first * moment_one + (1.0 - beta_first) * gradient
    two_new = beta_second * moment_two + (1.0 - beta_second) * gradient * gradient
    fix_first = 1.0 - beta_first**STEP
    fix_second = 1.0 - beta_second**STEP
    weight_new = weight_now - step_rate * (
        one_new / fix_first / (jnp.sqrt(two_new / fix_second) + adam_eps) + decay_value * weight_now
    )
    return (two_new, weight_new)


def body(count, inputs, cotangent, segments, norm_gains, *rest):
    masters, firsts, seconds = rest[0:7], rest[7:14], rest[14:21]
    gain_first, gain_second = rest[21:23]
    query_cols = HEADS * HEAD
    pair_cols = KV_HEADS * HEAD
    shapes = (
        (D, query_cols),
        (D, pair_cols),
        (D, pair_cols),
        (query_cols, D),
        (D, FF),
        (D, FF),
        (FF, D),
    )
    sizes = [master.shape[0] for master in masters]
    seqs, seq = inputs.shape[0], inputs.shape[1]
    wq, wk, wv = gather_group(masters[:3], shapes[:3], count)
    wo, wg, wu, wd = gather_group(masters[3:], shapes[3:], count)
    cosine, sine = rope_tables(doc_positions(segments))
    seg_col, seg_row = segments[:, :, None], segments[:, None, :]
    common = (inputs, norm_gains, seg_col, seg_row, cosine, sine, wq, wk, wv)
    q, k, v, lse, att = attention_forward(*common)
    flat = (seqs * seq, D)
    out, mid_back, att_back, grad_o, grad_g, grad_u, grad_d, gain_two = feed_forward(
        inputs.reshape(flat), att.reshape(flat), cotangent.reshape(flat), norm_gains, wo, wg, wu, wd
    )
    late = reduce_group((grad_o, grad_g, grad_u, grad_d), sizes[3:], count)
    whole_shape = inputs.shape
    x_back, grad_q, grad_k, grad_v, gain_one = attention_backward(
        *common, q, k, v, lse, att_back.reshape(whole_shape), mid_back.reshape(whole_shape)
    )
    early = reduce_group((grad_q, grad_k, grad_v), sizes[:3], count)
    gain_sum = jnp.concatenate([butterfly(gain_one, count), butterfly(gain_two, count)], axis=0)
    results = [out.reshape(whole_shape), x_back]
    for slot_index, gradient in enumerate(early + late):
        moment_new, weight_new = adam_step(
            masters[slot_index],
            gradient,
            firsts[slot_index],
            seconds[slot_index],
            learn_rate,
            decay_rate,
        )
        results.extend([gradient, moment_new, weight_new])
    gain_moment, gains_new = adam_step(
        norm_gains, gain_sum, gain_first, gain_second, gain_rate, 0.0
    )
    results.extend([gain_sum, gain_moment, gains_new])
    return tuple(results)


def solution(mesh):
    rows = P("dp", None, None)
    in_specs = (rows, rows, P("dp", None), P()) + (P("dp"),) * 21 + (P(), P())
    out_specs = (rows, rows) + (P("dp"),) * 21 + (P(), P(), P())
    return jax.shard_map(
        functools.partial(body, mesh.shape["dp"]),
        mesh=mesh,
        in_specs=in_specs,
        out_specs=out_specs,
        check_vma=False,
    )
```

time: 961 us -> 530 us (0.55)
  matrix products: 318 us -> 0 us
  Pallas kernels: 0 us -> 237 us
  blocking collectives: 209 us -> 0 us
  other arithmetic: 158 us -> 28.8 us
  waiting for transfers between devices: 187 us -> 127 us
  local copies, waits for them, and re-layouts: 64.1 us -> 95.2 us
  starting transfers between devices: 0.16 us -> 19.1 us
    dot_general x66 -> x0, matrix products: 318 us -> none  [the longest x4 51.2 us: attention_backward(): jnp.einsum('nqkgd,nskd->nkgqs', back_block, value_rows, preferred_element...]
    pallas_call x0 -> x3, Pallas kernels: none -> 237 us  [the longest x1 94.8 us: attention_backward(): pl.pallas_call(attend_back_kernel, grid=(seqs,), out_shape=[sds(x.shape,...]
    unnamed x5 -> x2, waiting for transfers between devices: 187 us -> 0.03 us
    all_gather x4 -> x0, blocking collectives: 171 us -> none  [the longest x1 44.7 us: body(): lax.all_gather(low_shards[0], 'dp', axis=0, tiled=True)]
    another operation x14 -> x2, other arithmetic: 70.4 us -> 0.77 us
    ppermute x0 -> x20, waiting for transfers between devices: none -> 69 us  [the longest x10 63.6 us: reduce_group(): got = lax.ppermute(give, 'dp', [(d, d ^ bit) for d in range(count)])]
    all_gather x3 -> x2, waiting for transfers between devices: 0.01 us -> 58.4 us  [gather_group(): rows = lax.all_gather(packed, 'dp', axis=0, tiled=False)]
    reduce_sum x5 -> x0, other arithmetic: 40.9 us -> none  [the longest x4 38.8 us: attention_forward(): row_total = jnp.sum(exp_terms, axis=-1, keepdims=True)]
  transfers between devices with their start and end apart: 4 -> 22, of which waited for: 1 -> 13; matrix products, arithmetic and copies ran while one was open for 22% -> 11% of each run, Pallas kernels for 0% -> 32%
where the time goes in v1:
time: 530 us; the launch traced here: 523 us
  Pallas kernels  237 us (45%)
  waiting for transfers between devices  127 us (24%)
  local copies, waits for them, and re-layouts  95.2 us (18%)
  other arithmetic  28.8 us (5%)
  starting transfers between devices  19.1 us (4%)
  between operations  14.9 us (3%)
    pallas_call x1, Pallas kernels, attention_backward(): pl.pallas_call(attend_back_kernel, grid=(seqs,), out_shape=[sds(x.shape,...  94.8 us
    pallas_call x1, Pallas kernels, attention_forward(): pl.pallas_call(attend_kernel, grid=(seqs,), out_shape=[sds(*o) for o in o...  72.4 us
    pallas_call x1, Pallas kernels, feed_forward(): pl.pallas_call(feed_kernel, grid=(tokens // BLOCK,), out_shape=[sds((toke...  70.1 us
    ppermute x10, waiting for transfers between devices, reduce_group(): got = lax.ppermute(give, 'dp', [(d, d ^ bit) for d in range(count)])  63.6 us
    all_gather x2, waiting for transfers between devices, gather_group(): rows = lax.all_gather(packed, 'dp', axis=0, tiled=False)  58.4 us
    reshape x7, local copies, waits for them, and re-layouts, gather_group(): result.append(rows[:, place:place + size].reshape(shape))  28.5 us
    unnamed x77, local copies, waits for them, and re-layouts  26.5 us
    reshape x7, local copies, waits for them, and re-layouts, reduce_group(): parts = [grad.reshape(count, size) for grad, size in zip(grads, sizes)]  18.2 us
  transfers between devices with their start and end apart: 22, of which 13 were waited for; matrix products, arithmetic and copies ran while one was open for 11% of the time, Pallas kernels for 32%

profile of v1, /device:TPU:0, one launch (start us, length us, event | category | flops | bytes accessed | tf_op | source)
XLA Modules:
  0.0 522.8 jit_solution(17436790613557294511)
XLA Ops:
  16.5 4.5 copy.98.x
  21.0 1.3 copy.100.seg_col
  22.4 2.6 copy.101
  25.0 3.7 fusion.6
  28.8 2.0 pad_maximum_fusion.2
  30.8 40.3 %all-gather.7.cloned.1.call-done = bf16[32,1,17280]{2,1,0:T(2,128)(2,1)} async-done(((bf16[1,1,17280]{2,1,0:T(2,128)(2,1)}), bf16[32,1,17280]{2,1,0:T(2,128)(2,1)}) %all-gather.7.cloned.1.call-update) | async-done | bytes 1105936 | tf_op jit(solution)/shard_map/all_gather | solution.py:336
  71.0 1.7 copy.138
  74.7 1.8 reshape.204.wq
  76.5 72.4 %attention_forward.1 = (bf16[2,9,1024,64]{3,2,1,0:T(8,128)(2,1)}, bf16[2,3,1024,64]{3,2,1,0:T(8,128)(2,1)}, bf16[2,3,1024,64]{3,2,1,0:T(8,128)(2,1)}, f32[2,9,1,1024]{3,2,1,0:T(1,128)}, bf16[2,1024,576]{2,1,0:T(8,128)(2,1)}) custom-call(bf16[2,1024,576]{2,1,0:T(8,128)(2,1)} %copy.98.x, f32[2,576]{1,0:T(2,128)} %gains.5, s32[2,1024,1]{2,1,0:T(8,128)} %copy.100.seg_col, ...), custom_call_target="tpu_custom_call" | custom-call | flops 60000002048 | bytes 20000000 | tf_op jit(solution)/shard_map/attention_forward/pallas_call | solution.py:257
  148.9 18.1 %all-gather.9.cloned.1.call-done = bf16[32,1,93312]{2,1,0:T(2,128)(2,1)} async-done(((bf16[1,1,93312]{2,1,0:T(2,128)(2,1)}), bf16[32,1,93312]{2,1,0:T(2,128)(2,1)}) %all-gather.9.cloned.1.call-update) | async-done | bytes 5971984 | tf_op jit(solution)/shard_map/all_gather | solution.py:336
  167.0 5.0 copy.135
  172.1 2.3 fusion.27
  175.3 2.6 reshape.212.wd
  177.8 4.9 reshape.210.wg
  182.7 15.6 %reshape.211.wu = bf16[576,1536]{1,0:T(8,128)(2,1)} reshape(bf16[32,27648]{1,0:T(8,128)(2,1)S(1)} %copy-done) | data formatting | bytes 3538944 | tf_op jit(solution)/shard_map/reshape | solution.py:341
  198.3 1.8 reshape.209.wo
  200.1 70.1 %feed_forward.1 = (bf16[2048,576]{1,0:T(8,128)(2,1)}, f32[2048,576]{1,0:T(8,128)}, bf16[2048,576]{1,0:T(8,128)(2,1)}, bf16[576,576]{1,0:T(8,128)(2,1)}, bf16[576...) custom-call(bf16[2048,576]{1,0:T(8,128)(2,1)} %bitcast.112, ...), custom_call_target="tpu_custom_call" | custom-call | flops 60000002048 | bytes 30000000 | tf_op jit(solution)/shard_map/feed_forward/pallas_call | solution.py:282
  270.2 4.1 reshape.223
  274.3 3.7 reshape.224
  278.1 3.0 reshape.225
  281.1 2.6 reshape.222
  283.7 4.7 pad_maximum_fusion
  288.4 7.1 %reshape_reshape.7 = bf16[16,2,729,128]{3,2,1,0:T(8,128)(2,1)} reshape(bf16[32,93312]{1,0:T(8,128)(2,1)} %pad_maximum_fusion) | data formatting | bytes 11943936 | tf_op jit(solution)/shard_map/reshape;reshape | solution.py:356
  295.5 2.0 constant_dynamic-slice_fusion.2
  297.5 2.8 copy.136
  300.6 94.8 %attention_backward.1 = (f32[2,1024,576]{2,1,0:T(8,128)}, bf16[576,576]{1,0:T(8,128)(2,1)}, bf16[576,192]{1,0:T(8,128)(2,1)}, bf16[576,192]{1,0:T(8,128)(2,1)}, f32[1,576]{1,0:T(1,128)}) custom-call(bf16[2,1024,576]{2,1,0:T(8,128)(2,1)} %copy.98.x, f32[2,576]{1,0:T(2,128)} %gains.5, s32[2,1024,1]{2,1,0:T(8,128)} %copy.100.seg_col, ...), custom_call_target="tpu_custom_call" | custom-call | flops 120000004096 | bytes 40000000 | tf_op jit(solution)/shard_map/attention_backward/pallas_call | solution.py:307
  395.5 2.1 reshape.216
  397.6 1.3 reshape.217
  402.2 3.5 fusion
  405.9 1.7 copy.137
  407.6 1.5 collective-permute-start.6
  411.7 37.0 %collective-permute-done.1 = bf16[8,135,128]{2,1,0:T(8,128)(2,1)} collective-permute-done((bf16[8,135,128]{2,1,0:T(8,128)(2,1)S(1)}, bf16[8,135,128]{2,1,0:T(8,128)(2,1)}, u32[]{:S(2)}, u32[]{:S(2)}) %collective-permute-start.1) | collective-permute-done | bytes 276512 | tf_op jit(solution)/shard_map/ppermute | solution.py:360
  450.5 1.6 collective-permute-start.2
  453.9 1.5 collective-permute-start.16
  455.4 1.5 collective-permute-done.11
  457.5 1.4 collective-permute-start.17
  459.0 1.5 collective-permute-done.12
  462.6 1.5 collective-permute-done.13
  464.1 1.7 collective-permute-start.14
  465.7 1.3 collective-permute-start.19
  467.1 5.7 %copy.116 = f32[2,1024,576]{1,2,0:T(8,128)} copy(f32[2,1024,576]{2,1,0:T(8,128)} %get-tuple-element.167) | data formatting | bytes 9437184
  472.8 4.3 copy.115
  478.3 1.7 fusion.1
  481.8 1.5 collective-permute-start.4
  484.0 2.7 collective-permute-done.4
  486.8 8.4 %collective-permute-done.7 = bf16[4,729,128]{2,0,1:T(4,128)(2,1)S(1)} collective-permute-done((bf16[4,729,128]{2,0,1:T(4,128)(2,1)S(1)}, bf16[4,729,128]{2,0,1:T(4,128)(2,1)S(1)}, u32[]{:S(2)}, u32[]{:S(2)}) %collective-permute-start.7) | collective-permute-done | bytes 746528 | tf_op jit(solution)/shard_map/ppermute | solution.py:360
  497.1 8.1 %collective-permute-done.8 = bf16[2,729,128]{2,1,0:T(8,128)(2,1)S(1)} collective-permute-done((bf16[2,729,128]{2,1,0:T(8,128)(2,1)S(1)}, bf16[2,729,128]{2,1,0:T(8,128)(2,1)S(1)}, u32[]{:S(2)}, u32[]{:S(2)}) %collective-permute-start.8) | collective-permute-done | bytes 373280 | tf_op jit(solution)/shard_map/ppermute | solution.py:360
  507.1 6.8 %collective-permute-done.9 = bf16[1,729,128]{2,1,0:T(8,128)(2,1)S(1)} collective-permute-done((bf16[1,729,128]{2,1,0:T(8,128)(2,1)S(1)}, bf16[1,729,128]{2,1,0:T(8,128)(2,1)S(1)}, u32[]{:S(2)}, u32[]{:S(2)}) %collective-permute-start.9) | collective-permute-done | bytes 186656 | tf_op jit(solution)/shard_map/ppermute | solution.py:360
  (160 shorter events, 33.9 us)
Async XLA Ops:
  7.2 7.6 %copy-start.12 = (s32[2,1024]{1,0:T(2,128)S(1)}, s32[2,1024]{1,0:T(2,128)}, u32[]{:S(2)}) copy-start(s32[2,1024]{1,0:T(2,128)} %param.29) | copy-start | bytes 24580
  7.2 63.8 %all-gather.7.cloned.1.call-start = ((), (), s32[]{:S(2)}) async-start(), calls=%async_computation | async-start | bytes 2280960 | tf_op jit(solution)/shard_map/all_gather | solution.py:336
  10.2 156.8 %all-gather.9.cloned.1.call-start = ((), (), s32[]{:S(2)}) async-start(), calls=%async_computation.1 | async-start | bytes 12317184 | tf_op jit(solution)/shard_map/all_gather | solution.py:336
  16.5 5.8 %copy-start.4 = (bf16[2,1024,576]{1,2,0:T(8,128)(2,1)S(1)}, bf16[2,1024,576]{1,2,0:T(8,128)(2,1)}, u32[]{:S(2)}) copy-start(bf16[2,1024,576]{1,2,0:T(8,128)(2,1)} %param.28) | copy-start | bytes 7077892
  182.7 15.6 %copy-start.3 = (bf16[32,10368]{1,0:T(8,128)(2,1)S(1)}, bf16[32,10368]{1,0:T(8,128)(2,1)}, u32[]{:S(2)}) copy-start(bf16[32,10368]{1,0:T(8,128)(2,1)} %slice.104) | copy-start | bytes 1990660
  300.4 101.8 %collective-permute-start.5 = (bf16[16,729,128]{2,0,1:T(8,128)(2,1)}, bf16[16,729,128]{2,0,1:T(8,128)(2,1)}, u32[]{:S(2)}, u32[]{:S(2)}) collective-permute-start(bf16[16,729,128]{2,0,1:T(8,128)(2,1)} %bitcast.95), channel_id=1, source_target_pairs={{0,1},{1,0},{2,3},{3,2},{4,5},{5,4},{6,7},{7,6},{8,9},{9,8},{10,11... | collective-permute-start | bytes 8957960 | tf_op jit(solution)/shard_map/ppermute | solution.py:360
  401.9 7.1 %collective-permute-start = (bf16[16,135,128]{2,0,1:T(8,128)(2,1)}, bf16[16,135,128]{2,0,1:T(8,128)(2,1)}, u32[]{:S(2)}, u32[]{:S(2)}) collective-permute-start(bf16[16,135,128]{2,0,1:T(8,128)(2,1)} %bitcast.98), channel_id=1, source_target_pairs={{0,1},{1,0},{2,3},{3,2},{4,5},{5,4},{6,7},{7,6},{8,9},{9,8},{10,11... | collective-permute-start | bytes 1658888 | tf_op jit(solution)/shard_map/ppermute | solution.py:360
  407.6 44.6 %copy-start.33 = (f32[1,576]{1,0:T(1,128)S(1)}, f32[1,576]{1,0:T(1,128)}, u32[]{:S(2)}) copy-start(f32[1,576]{1,0:T(1,128)} %get-tuple-element.60) | copy-start | bytes 6916
  407.6 44.6 %copy-start.32 = (f32[1,576]{1,0:T(1,128)S(1)}, f32[1,576]{1,0:T(1,128)}, u32[]{:S(2)}) copy-start(f32[1,576]{1,0:T(1,128)} %get-tuple-element.61) | copy-start | bytes 6916
  407.6 70.8 %collective-permute-start.6 = (bf16[8,729,128]{2,0,1:T(8,128)(2,1)}, bf16[8,729,128]{2,0,1:T(8,128)(2,1)}, u32[]{:S(2)}, u32[]{:S(2)}) collective-permute-start(bf16[8,729,128]{2,0,1:T(8,128)(2,1)} %bitcast.96), channel_id=1, source_target_pairs={{0,2},{1,3},{2,0},{3,1},{4,6},{5,7},{6,4},{7,5},{8,10},{9,11},{10,... | collective-permute-start | bytes 4478984 | tf_op jit(solution)/shard_map/ppermute | solution.py:360
  411.1 37.6 %collective-permute-start.1 = (bf16[8,135,128]{2,1,0:T(8,128)(2,1)S(1)}, bf16[8,135,128]{2,1,0:T(8,128)(2,1)}, u32[]{:S(2)}, u32[]{:S(2)}) collective-permute-start(bf16[8,135,128]{2,1,0:T(8,128)(2,1)S(1)} %dynamic-slice_bitcast_fusion.2), channel_id=1, source_target_pairs={{0,2},{1,3},{2,0},{3,1},{4,6},{5,7},{6,4},{7,5},{8,10},{9,11},{10,... | collective-permute-start | bytes 829448 | tf_op jit(solution)/shard_map/ppermute | solution.py:360
  450.5 26.6 %collective-permute-start.2 = (bf16[4,135,128]{2,1,0:T(8,128)(2,1)}, bf16[4,135,128]{2,1,0:T(8,128)(2,1)S(1)}, u32[]{:S(2)}, u32[]{:S(2)}) collective-permute-start(bf16[4,135,128]{2,1,0:T(8,128)(2,1)} %dynamic-slice_bitcast_fusion.3), channel_id=1, source_target_pairs={{0,4},{1,5},{2,6},{3,7},{4,0},{5,1},{6,2},{7,3},{8,12},{9,13},{10,... | collective-permute-start | bytes 414728 | tf_op jit(solution)/shard_map/ppermute | solution.py:360
  452.1 1.2 collective-permute-start.10
  452.1 1.8 collective-permute-start.15
  453.3 3.6 collective-permute-start.11
  453.9 3.7 collective-permute-start.16
  456.9 3.6 collective-permute-start.12
  457.5 4.0 collective-permute-start.17
  460.5 3.6 collective-permute-start.13
  461.6 4.2 collective-permute-start.18
  464.1 13.0 %collective-permute-start.14 = (f32[1,576]{1,0:T(1,128)S(1)}, f32[1,576]{1,0:T(1,128)S(1)}, u32[]{:S(2)}, u32[]{:S(2)}) collective-permute-start(f32[1,576]{1,0:T(1,128)S(1)} %add.265), channel_id=1, source_target_pairs={{0,16},{1,17},{2,18},{3,19},{4,20},{5,21},{6,22},{7,23},{8,24},{9,... | collective-permute-start | bytes 6920 | tf_op jit(solution)/shard_map/ppermute | solution.py:377
  465.7 11.3 %collective-permute-start.19 = (f32[1,576]{1,0:T(1,128)S(1)}, f32[1,576]{1,0:T(1,128)S(1)}, u32[]{:S(2)}, u32[]{:S(2)}) collective-permute-start(f32[1,576]{1,0:T(1,128)S(1)} %add.270), channel_id=1, source_target_pairs={{0,16},{1,17},{2,18},{3,19},{4,20},{5,21},{6,22},{7,23},{8,24},{9,... | collective-permute-start | bytes 6920 | tf_op jit(solution)/shard_map/ppermute | solution.py:377
  477.2 4.6 collective-permute-start.3
  480.1 16.3 %copy-start.10 = (f32[10368]{0:T(1024)S(1)}, f32[10368]{0:T(1024)}, u32[]{:S(2)}) copy-start(f32[10368]{0:T(1024)} %param.31) | copy-start | bytes 124420
  480.1 16.3 %copy-start.21 = (f32[10368]{0:T(1024)S(1)}, f32[10368]{0:T(1024)}, u32[]{:S(2)}) copy-start(f32[10368]{0:T(1024)} %param.38) | copy-start | bytes 124420
  480.1 16.3 %copy-start.22 = (f32[10368]{0:T(1024)S(1)}, f32[10368]{0:T(1024)}, u32[]{:S(2)}) copy-start(f32[10368]{0:T(1024)} %param.45) | copy-start | bytes 124420
  480.6 14.7 %collective-permute-start.7 = (bf16[4,729,128]{2,0,1:T(4,128)(2,1)S(1)}, bf16[4,729,128]{2,0,1:T(4,128)(2,1)S(1)}, u32[]{:S(2)}, u32[]{:S(2)}) collective-permute-start(bf16[4,729,128]{2,0,1:T(4,128)(2,1)S(1)} %copy.111), channel_id=1, source_target_pairs={{0,4},{1,5},{2,6},{3,7},{4,0},{5,1},{6,2},{7,3},{8,12},{9,13},{10,... | collective-permute-start | bytes 2239496 | tf_op jit(solution)/shard_map/ppermute | solution.py:360
  481.8 4.9 collective-permute-start.4
  486.8 19.7 %copy-start.19 = (f32[3456]{0:T(1024)S(1)}, f32[3456]{0:T(1024)}, u32[]{:S(2)}) copy-start(f32[3456]{0:T(1024)} %param.33) | copy-start | bytes 41476
  486.8 19.7 %copy-start.20 = (f32[3456]{0:T(1024)S(1)}, f32[3456]{0:T(1024)}, u32[]{:S(2)}) copy-start(f32[3456]{0:T(1024)} %param.32) | copy-start | bytes 41476
  486.8 19.7 %copy-start.25 = (f32[3456]{0:T(1024)S(1)}, f32[3456]{0:T(1024)}, u32[]{:S(2)}) copy-start(f32[3456]{0:T(1024)} %param.40) | copy-start | bytes 41476
  486.8 19.7 %copy-start.26 = (f32[3456]{0:T(1024)S(1)}, f32[3456]{0:T(1024)}, u32[]{:S(2)}) copy-start(f32[3456]{0:T(1024)} %param.47) | copy-start | bytes 41476
  486.8 19.7 %copy-start.27 = (f32[3456]{0:T(1024)S(1)}, f32[3456]{0:T(1024)}, u32[]{:S(2)}) copy-start(f32[3456]{0:T(1024)} %param.46) | copy-start | bytes 41476
  486.8 19.7 %copy-start.28 = (f32[3456]{0:T(1024)S(1)}, f32[3456]{0:T(1024)}, u32[]{:S(2)}) copy-start(f32[3456]{0:T(1024)} %param.39) | copy-start | bytes 41476
  495.4 18.6 %copy-start.11 = (f32[10368]{0:T(1024)S(1)}, f32[10368]{0:T(1024)}, u32[]{:S(2)}) copy-start(f32[10368]{0:T(1024)} %param.34) | copy-start | bytes 124420
  495.4 18.6 %copy-start.23 = (f32[10368]{0:T(1024)S(1)}, f32[10368]{0:T(1024)}, u32[]{:S(2)}) copy-start(f32[10368]{0:T(1024)} %param.41) | copy-start | bytes 124420
  495.4 18.6 %copy-start.24 = (f32[10368]{0:T(1024)S(1)}, f32[10368]{0:T(1024)}, u32[]{:S(2)}) copy-start(f32[10368]{0:T(1024)} %param.48) | copy-start | bytes 124420
  495.4 19.3 %copy-start.7 = (f32[27648]{0:T(1024)S(1)}, f32[27648]{0:T(1024)}, u32[]{:S(2)}) copy-start(f32[27648]{0:T(1024)} %param.37) | copy-start | bytes 331780
  495.4 19.3 %copy-start.8 = (f32[27648]{0:T(1024)S(1)}, f32[27648]{0:T(1024)}, u32[]{:S(2)}) copy-start(f32[27648]{0:T(1024)} %param.36) | copy-start | bytes 331780
  495.4 19.3 %copy-start.9 = (f32[27648]{0:T(1024)S(1)}, f32[27648]{0:T(1024)}, u32[]{:S(2)}) copy-start(f32[27648]{0:T(1024)} %param.35) | copy-start | bytes 331780
  495.4 19.3 %copy-start.13 = (f32[27648]{0:T(1024)S(1)}, f32[27648]{0:T(1024)}, u32[]{:S(2)}) copy-start(f32[27648]{0:T(1024)} %param.44) | copy-start | bytes 331780
  495.4 19.3 %copy-start.14 = (f32[27648]{0:T(1024)S(1)}, f32[27648]{0:T(1024)}, u32[]{:S(2)}) copy-start(f32[27648]{0:T(1024)} %param.51) | copy-start | bytes 331780
  495.5 19.3 %copy-start.15 = (f32[27648]{0:T(1024)S(1)}, f32[27648]{0:T(1024)}, u32[]{:S(2)}) copy-start(f32[27648]{0:T(1024)} %param.50) | copy-start | bytes 331780
  495.5 19.3 %copy-start.16 = (f32[27648]{0:T(1024)S(1)}, f32[27648]{0:T(1024)}, u32[]{:S(2)}) copy-start(f32[27648]{0:T(1024)} %param.43) | copy-start | bytes 331780
  495.5 19.3 %copy-start.17 = (f32[27648]{0:T(1024)S(1)}, f32[27648]{0:T(1024)}, u32[]{:S(2)}) copy-start(f32[27648]{0:T(1024)} %param.49) | copy-start | bytes 331780
  495.5 19.3 %copy-start.18 = (f32[27648]{0:T(1024)S(1)}, f32[27648]{0:T(1024)}, u32[]{:S(2)}) copy-start(f32[27648]{0:T(1024)} %param.42) | copy-start | bytes 331780
  495.5 9.7 %collective-permute-start.8 = (bf16[2,729,128]{2,1,0:T(8,128)(2,1)S(1)}, bf16[2,729,128]{2,1,0:T(8,128)(2,1)S(1)}, u32[]{:S(2)}, u32[]{:S(2)}) collective-permute-start(bf16[2,729,128]{2,1,0:T(8,128)(2,1)S(1)} %dynamic-slice_bitcast_fusion.1), channel_id=1, source_target_pairs={{0,8},{1,9},{2,10},{3,11},{4,12},{5,13},{6,14},{7,15},{8,0},{9,1},... | collective-permute-start | bytes 1119752 | tf_op jit(solution)/shard_map/ppermute | solution.py:360
  505.4 8.6 %collective-permute-start.9 = (bf16[1,729,128]{2,1,0:T(8,128)(2,1)S(1)}, bf16[1,729,128]{2,1,0:T(8,128)(2,1)S(1)}, u32[]{:S(2)}, u32[]{:S(2)}) collective-permute-start(bf16[1,729,128]{2,1,0:T(8,128)(2,1)S(1)} %constant_dynamic-slice_fusion), channel_id=1, source_target_pairs={{0,16},{1,17},{2,18},{3,19},{4,20},{5,21},{6,22},{7,23},{8,24},{9,... | collective-permute-start | bytes 559880 | tf_op jit(solution)/shard_map/ppermute | solution.py:360
  (8 other events, 24.4 us)
Sparse Core Ops, SparseCore 0:
  11.5 59.4 all-gather.6
  74.4 92.5 all-gather.8
